TPU v7x, 32 devices: a whole 2x2x4 slice. The times are simulated.
32 devices in a mesh: tile: 4 (over z), tensor: 8 (over y, x, core).
Axes of the slice: x: 2, y: 2, z: 4, core: 2. Of those that a mesh axis runs over, the one named last changes fastest.
Arguments:
- image_hidden: bfloat16 [8, 32, 32, 3072], P(None, 'tile', 'tensor'), may hold values from -6 to 6
- text_hidden: bfloat16 [8, 512, 3072], P(None, ('tile', 'tensor')), may hold values from -6 to 6
- latents: float32 [8, 32, 2048], P(None, 'tile', 'tensor'), may hold values from -6 to 6
- step_index: int32 [8], replicated, may hold values from 0 to 27
- anchor: int32 [8, 2], replicated, may hold values from 0 to 63
- text_len: int32 [8], replicated, may hold values from 64 to 512
- mod_image: float32 [8, 3, 3072], replicated, may hold values from -3 to 3
- mod_text: float32 [8, 3, 3072], replicated, may hold values from -3 to 3
- mod_mlp: float32 [8, 3, 3072], replicated, may hold values from -3 to 3
- mod_final: float32 [8, 2, 3072], replicated, may hold values from -3 to 3
- qkv_image: bfloat16 [3072, 3, 2048], P(None, None, 'tensor'), may hold values from -0.109375 to 0.109375
- qkv_text: bfloat16 [3072, 3, 2048], P(None, None, 'tensor'), may hold values from -0.109375 to 0.109375
- proj_image: bfloat16 [2048, 3072], P('tensor'), may hold values from -0.125 to 0.125
- proj_text: bfloat16 [2048, 3072], P('tensor'), may hold values from -0.125 to 0.125
- qk_gain: float32 [2, 2, 128], replicated, may hold values from 0.5 to 10
- mlp_expand: bfloat16 [3072, 6144], P(None, 'tensor'), may hold values from -0.109375 to 0.109375
- mlp_reduce: bfloat16 [6144, 3072], P('tensor'), may hold values from -0.078125 to 0.078125
- final_weight: bfloat16 [3072, 64], replicated, may hold values from -0.109375 to 0.109375
Outputs:
- image_out: bfloat16 [8, 32, 32, 3072], P(None, 'tile', 'tensor')
- text_out: bfloat16 [8, 512, 3072], P(None, ('tile', 'tensor'))
- latents_ext: float32 [8, 40, 2048], P(None, 'tile', 'tensor')
Inputs may be any that keep to these rules, and one draw needn't show every extreme that they name: text_len gives each request's live text tokens; slots at or past it take no part as keys. step_index is a step of the 28-step plan.
All inputs are finite; a program needn't handle non-finite values.
Results may differ from a plain program's by a relative error of at most 0.0085.
The roundings to bfloat16 on the way count: a program that leaves them out, or rounds other values in their place, can miss the bound.
Values may be sent and summed in bfloat16 or wider, within the bound.
A program may use at most 128 MiB of HBM per device.

v0:
```python
import math

import jax
import jax.numpy as jnp
from jax import lax
from jax.sharding import PartitionSpec as P

HEAD_DIM = 128
GRID = 32
NSTEPS = 28


norm_eps = 1e-06
time_shift = 3.0


def padded(value, sides, width):
    for axis, dim in sides:
        size, length = (lax.axis_size(axis), value.shape[dim])
        up = [(i, (i + 1) % size) for i in range(size - 1)]
        down = [(j, i) for i, j in up]
        last = lax.slice_in_dim(value, length - width, length, axis=dim)
        leading = lax.slice_in_dim(value, 0, width, axis=dim)
        before = lax.ppermute(last, axis, up)
        after = lax.ppermute(leading, axis, down)
        value = jnp.concatenate([before, value, after], axis=dim)
    return value


def layer_norm(values):
    average = jnp.mean(values, -1, keepdims=True)
    centred = values - average
    spread = jnp.mean(centred * centred, -1, keepdims=True)
    return centred * lax.rsqrt(spread + norm_eps)


def modulate(hidden, shift, stretch):
    normed = layer_norm(hidden.astype(jnp.float32))
    return ((1.0 + stretch) * normed + shift).astype(jnp.bfloat16)


def rope_tables(row_ids, col_ids):
    pair_index = jnp.arange(64, dtype=jnp.int32)
    row_rank = (pair_index - 8).astype(jnp.float32)
    col_rank = (pair_index - 36).astype(jnp.float32)
    log_base = math.log(10000.0)
    row_freq = jnp.where(
        (pair_index >= 8) & (pair_index < 36), jnp.exp(-2.0 * row_rank / 56.0 * log_base), 0.0
    )
    col_freq = jnp.where(pair_index >= 36, jnp.exp(-2.0 * col_rank / 56.0 * log_base), 0.0)
    angles = row_ids[..., None] * row_freq + col_ids[..., None] * col_freq
    angles = jnp.repeat(angles, 2, axis=-1)
    sign_table = jnp.where(jnp.arange(128, dtype=jnp.int32) % 2 == 0, -1.0, 1.0).astype(jnp.float32)
    return (jnp.cos(angles), jnp.sin(angles) * sign_table)


def rotate(values, cos_table, sin_table):
    paired = values.reshape(values.shape[:-1] + (values.shape[-1] // 2, 2))
    swapped = jnp.flip(paired, -1).reshape(values.shape)
    return values * cos_table + swapped * sin_table


def head_norm(projected, head_gain):
    squares = jnp.mean(projected * projected, -1, keepdims=True)
    return projected * lax.rsqrt(squares + norm_eps) * head_gain


def sigma_of(step_float):
    level = 1.0 - step_float / NSTEPS
    return time_shift * level / (1.0 + (time_shift - 1.0) * level)


def key_usable(text_len, key_count, text_tile, block_len):
    key_pos = jnp.arange(key_count, dtype=jnp.int32)
    owner_tile = key_pos // block_len
    offset = key_pos % block_len
    text_pos = owner_tile * text_tile + offset
    return jnp.logical_or(offset[None, :] >= text_tile, text_pos[None, :] < text_len[:, None])


def per_device(
    image_hidden,
    text_hidden,
    latents,
    step_index,
    anchor,
    text_len,
    mod_image,
    mod_text,
    mod_mlp,
    mod_final,
    qkv_image,
    qkv_text,
    proj_image,
    proj_text,
    qk_gain,
    mlp_expand,
    mlp_reduce,
    final_weight,
):
    requests, tile_rows, tile_cols, model_width = image_hidden.shape
    local_cols = qkv_image.shape[2]
    local_heads = local_cols // HEAD_DIM
    local_units = mlp_expand.shape[1]
    image_all, text_all = (
        lax.all_gather(image_hidden, "tensor", axis=2, tiled=True),
        lax.all_gather(text_hidden, "tensor", axis=1, tiled=True),
    )
    image_mod = modulate(image_all, mod_image[:, 0, None, None, :], mod_image[:, 1, None, None, :])
    text_mod = modulate(text_all, mod_text[:, 0, None, :], mod_text[:, 1, None, :])
    text_tile = text_mod.shape[1]
    image_count = tile_rows * GRID
    block_len = text_tile + image_count
    tile_index = lax.axis_index("tile")
    token_index = jnp.arange(image_count, dtype=jnp.int32)
    row_ids = (anchor[:, 0:1] + tile_index * tile_rows + token_index[None, :] // GRID).astype(
        jnp.float32
    )
    col_ids = (anchor[:, 1:2] + token_index[None, :] % GRID).astype(jnp.float32)
    cos_table, sin_table = rope_tables(row_ids, col_ids)
    cos_table = cos_table[:, :, None, :]
    sin_table = sin_table[:, :, None, :]
    image_qkv = jnp.dot(
        image_mod.reshape(requests * image_count, model_width),
        qkv_image.reshape(model_width, 3 * local_cols),
        preferred_element_type=jnp.float32,
    ).reshape(requests, image_count, 3, local_heads, HEAD_DIM)
    text_qkv = jnp.dot(
        text_mod.reshape(requests * text_tile, model_width),
        qkv_text.reshape(model_width, 3 * local_cols),
        preferred_element_type=jnp.float32,
    ).reshape(requests, text_tile, 3, local_heads, HEAD_DIM)
    query = jnp.concatenate(
        [
            head_norm(text_qkv[:, :, 0], qk_gain[1, 0]).astype(jnp.bfloat16),
            rotate(head_norm(image_qkv[:, :, 0], qk_gain[0, 0]), cos_table, sin_table).astype(
                jnp.bfloat16
            ),
        ],
        1,
    )
    keys = jnp.concatenate(
        [
            head_norm(text_qkv[:, :, 1], qk_gain[1, 1]).astype(jnp.bfloat16),
            rotate(head_norm(image_qkv[:, :, 1], qk_gain[0, 1]), cos_table, sin_table).astype(
                jnp.bfloat16
            ),
        ],
        1,
    )
    values = jnp.concatenate([text_qkv[:, :, 2], image_qkv[:, :, 2]], 1).astype(jnp.bfloat16)
    score_scale = 1.0 / math.sqrt(HEAD_DIM)
    keys_all, values_all = (
        lax.all_gather(keys, "tile", axis=1, tiled=True),
        lax.all_gather(values, "tile", axis=1, tiled=True),
    )
    usable = key_usable(text_len, keys_all.shape[1], text_tile, block_len)[:, None, None, :]
    scores = (
        jnp.einsum("rqhd,rkhd->rhqk", query, keys_all, preferred_element_type=jnp.float32)
        * score_scale
    )
    row_top = jnp.max(jnp.where(usable, scores, -jnp.inf), -1, keepdims=True)
    weights_raw = jnp.where(usable, jnp.exp(scores - row_top), 0.0)
    weight_sum = jnp.sum(weights_raw, -1, keepdims=True)
    accum = jnp.einsum(
        "rhqk,rkhd->rhqd",
        weights_raw.astype(jnp.bfloat16),
        values_all,
        preferred_element_type=jnp.float32,
    )
    attended = (accum / weight_sum).transpose(0, 2, 1, 3).astype(jnp.bfloat16)
    text_term = jnp.dot(
        attended[:, :text_tile].reshape(requests * text_tile, local_cols),
        proj_text,
        preferred_element_type=jnp.float32,
    ).reshape(requests, text_tile, model_width)
    image_term = jnp.dot(
        attended[:, text_tile:].reshape(requests * image_count, local_cols),
        proj_image,
        preferred_element_type=jnp.float32,
    ).reshape(requests, tile_rows, GRID, model_width)
    image_gate = mod_image[:, 2, None, None, :]
    image_sum, text_sum = (
        lax.psum_scatter(image_term, "tensor", scatter_dimension=2, tiled=True),
        lax.psum_scatter(text_term, "tensor", scatter_dimension=1, tiled=True),
    )
    image_mid = (image_hidden.astype(jnp.float32) + image_gate * image_sum).astype(jnp.bfloat16)
    mlp_mod = modulate(image_mid, mod_mlp[:, 0, None, None, :], mod_mlp[:, 1, None, None, :])
    piece = lax.all_gather(mlp_mod, "tensor", axis=2, tiled=True)
    grown = jnp.dot(piece.reshape(-1, model_width), mlp_expand, preferred_element_type=jnp.float32)
    activated = (
        jax.nn.gelu(grown, approximate=True)
        .astype(jnp.bfloat16)
        .reshape(piece.shape[:-1] + (local_units,))
    )
    text_out = (text_hidden.astype(jnp.float32) + mod_text[:, 2, None, :] * text_sum).astype(
        jnp.bfloat16
    )
    mlp_term = jnp.dot(
        activated.reshape(requests * image_count, local_units),
        mlp_reduce,
        preferred_element_type=jnp.float32,
    ).reshape(requests, tile_rows, GRID, model_width)
    mlp_sum = lax.psum_scatter(mlp_term, "tensor", scatter_dimension=2, tiled=True)
    image_out = (image_mid.astype(jnp.float32) + mod_mlp[:, 2, None, None, :] * mlp_sum).astype(
        jnp.bfloat16
    )
    final_in = modulate(image_out, mod_final[:, 0, None, None, :], mod_final[:, 1, None, None, :])
    velocity = jnp.dot(
        final_in.reshape(requests * tile_rows * tile_cols, model_width),
        final_weight,
        preferred_element_type=jnp.float32,
    ).reshape(requests, tile_rows, tile_cols * final_weight.shape[1])
    step_float = step_index.astype(jnp.float32)
    time_delta = sigma_of(step_float + 1.0) - sigma_of(step_float)
    latents_next = latents + time_delta[:, None, None] * velocity
    latents_ext = padded(latents_next, (("tile", 1),), 1)
    return (image_out, text_out, latents_ext)


def solution(mesh):
    return jax.shard_map(
        per_device,
        mesh=mesh,
        in_specs=(
            P(None, "tile", "tensor", None),
            P(None, ("tile", "tensor"), None),
            P(None, "tile", "tensor"),
            P(),
            P(),
            P(),
            P(),
            P(),
            P(),
            P(),
            P(None, None, "tensor"),
            P(None, None, "tensor"),
            P("tensor", None),
            P("tensor", None),
            P(),
            P(None, "tensor"),
            P("tensor", None),
            P(),
        ),
        out_specs=(
            P(None, "tile", "tensor", None),
            P(None, ("tile", "tensor"), None),
            P(None, "tile", "tensor"),
        ),
        check_vma=False,
    )
```

profile of v0, /device:TPU:0, one launch (start us, length us, event | category | flops | bytes accessed | tf_op | source)
XLA Modules:
  0.0 1097.8 jit_solution(2690933236105711855)
XLA Ops:
  8.0 3.0 copy.66
  11.5 1.9 fusion.76
  13.8 1.7 cos.12
  15.9 1.8 sin.12
  17.7 6.9 copy.70
  24.6 6.8 copy.67
  31.4 1.4 broadcast_multiply_fusion
  32.8 1.6 slice_bitcast_fusion.3
  34.4 23.8 %all-gather.6.cloned.1.call-done = bf16[8,128,3072]{2,1,0:T(8,128)(2,1)} async-done(((bf16[8,16,3072]{2,1,0:T(8,128)(2,1)}), bf16[8,128,3072]{2,1,0:T(8,128)(2,1)}) %all-gather.6.cloned.1.call-update) | async-done | bytes 6291472 | tf_op jit(solution)/shard_map/all_gather | solution.py:107
  58.2 3.8 convert_reduce_fusion.1
  62.8 1.8 fusion.20
  65.1 5.8 fusion.33
  71.6 1.0 copy-done.4
  72.5 1.8 multiply_convert_fusion.1
  74.3 1.0 copy.73
  75.4 57.5 %all-gather.8.cloned.1.call-done = bf16[8,8,32,3072]{3,1,0,2:T(8,128)(2,1)} async-done(((bf16[8,8,4,3072]{3,1,0,2:T(8,128)(2,1)}), bf16[8,8,32,3072]{3,1,0,2:T(8,128)(2,1)}) %all-gather.8.cloned.1.call-update) | async-done | bytes 12582928 | tf_op jit(solution)/shard_map/all_gather | solution.py:106
  132.8 17.6 %convert_reduce_fusion = f32[8,8,32]{2,1,0:T(8,128)S(1)} fusion(bf16[8,8,32,3072]{3,1,0,2:T(8,128)(2,1)} %all-gather.8.cloned.1.call-done), kind=kLoop, calls=%fused_computation.6 | loop fusion | flops 12580864 | bytes 12591104 | tf_op jit(solution)/shard_map/reduce_sum | solution.py:31
  150.5 19.0 %fusion.9 = f32[8,8,32]{2,1,0:T(8,128)} fusion(f32[8,8,32]{2,1,0:T(8,128)S(1)} %broadcast_multiply_fusion.1, bf16[8,8,32,3072]{3,1,0,2:T(8,128)(2,1)} %all-gather.8.cloned.1.call-done), kind=kLoop, calls=%fused_computation.10 | loop fusion | flops 25163776 | bytes 12599296 | tf_op jit(solution)/shard_map/reduce_sum | solution.py:33
  169.5 0.8 add_rsqrt_fusion
  170.3 30.5 %fusion.12 = bf16[8,8,32,3072]{3,2,1,0:T(8,128)(2,1)S(1)} fusion(f32[8,3072]{1,0:T(8,128)S(1)} %get-tuple-element.35, f32[8,8,32]{2,1,0:T(8,128)S(1)} %add_rsqrt_fusion, f32[8,8,32]{2,1,0:T(8,128)S(1)} %broadcast_multiply_fusion.1, f32[8,3072]{1,0:T(8,128)S(1)} %get-tuple-element.36, bf16[8,8,32,3072]{3,1,0,2:T(8,128)(2,1)} %all-gather.8.cloned.1.call-done), kind=kLoop, calls=%fused_computation.13 | loop fusion | flops 37748736 | bytes 25378816 | tf_op jit(solution)/shard_map/convert_element_type | solution.py:39
  200.9 9.9 fusion.110
  211.2 2.7 slice_bitcast_fusion
  213.9 0.9 copy-done.2
  214.8 3.5 squeeze.26
  218.3 4.0 multiply_multiply_fusion.2
  222.3 10.9 rev.7
  233.2 3.7 reshape.396
  236.9 3.6 squeeze.29
  240.5 4.0 multiply_multiply_fusion.1
  244.5 10.9 rev.8
  255.4 3.6 reshape.397
  259.0 6.1 fusion.59
  265.2 1.4 pad_maximum_fusion.1
  266.6 1.3 fusion.74
  268.3 1.8 fusion.71
  270.0 1.4 pad_maximum_fusion.2
  271.9 110.1 %all-gather.10.cloned.1.call-done = bf16[8,1536,2,128]{1,3,2,0:T(8,128)(2,1)} async-done(((bf16[8,384,2,128]{1,3,2,0:T(8,128)(2,1)}), bf16[8,1536,2,128]{1,3,2,0:T(8,128)(2,1)}) %all-gather.10.cloned.1.call-update) | async-done | bytes 6291472 | tf_op jit(solution)/shard_map/all_gather | solution.py:154
  382.1 20.7 %fusion.107 = (f32[8,2,384]{2,1,0:T(2,128)S(1)}, bf16[8,2,384,1536]{3,2,1,0:T(8,128)(2,1)}) fusion(bf16[8,1536,2,128]{1,3,2,0:T(8,128)(2,1)} %all-gather.10.cloned.1.call-done, pred[8,1536]{1,0:T(8,128)(4,1)S(1)} %compare_or_fusion, bf16[8,256,2,128]{1,3,2,0:T(8,128)(2,1)} %get-tuple-element.22, bf16[8,128,2,128]{1,3,2,0:T(8,128)(2,1)S(1)} %copy.72), kind=kOutput, calls=%fused_computation.185 | convolution fusion | flops 4904191488 | bytes 26775552 | tf_op jit(solution)/shard_map/sub | solution.py:163
  402.8 94.9 %all-gather.12.cloned.1.call-done = bf16[8,1536,2,128]{1,3,2,0:T(8,128)(2,1)} async-done(((bf16[8,384,2,128]{1,3,2,0:T(8,128)(2,1)}), bf16[8,1536,2,128]{1,3,2,0:T(8,128)(2,1)}) %all-gather.12.cloned.1.call-update) | async-done | bytes 6291472 | tf_op jit(solution)/shard_map/all_gather | solution.py:155
  497.7 11.1 %fusion.50 = bf16[8,384,2,128]{1,3,2,0:T(8,128)(2,1)S(1)} fusion(bf16[8,1536,2,128]{1,3,2,0:T(8,128)(2,1)} %all-gather.12.cloned.1.call-done, bf16[8,2,384,1536]{3,2,1,0:T(8,128)(2,1)} %get-tuple-element.50, f32[8,384,2]{1,2,0:T(2,128)S(1)} %bitcast.154), kind=kOutput, calls=%fused_computation.58 | convolution fusion | flops 2417491968 | bytes 26763264 | tf_op jit(solution)/shard_map/rhqk,rkhd->rhqd/dot_general | solution.py:165
  508.8 1.1 copy-done.7
  510.0 2.0 copy.77
  512.0 1.7 dot_general.53
  513.8 10.4 fusion.69
  524.3 0.9 copy-done.12
  525.2 154.3 %reduce-scatter.4.cloned.1.call-done = f32[8,8,4,3072]{3,1,0,2:T(8,128)} async-done(((f32[8,8,32,3072]{3,1,0,2:T(8,128)}), f32[8,8,4,3072]{3,1,0,2:T(8,128)}) %reduce-scatter.4.cloned.1.call-update) | async-done | bytes 3145744 | tf_op jit(solution)/shard_map/reduce_scatter | solution.py:184
  679.5 3.3 convert_reduce_fusion.2
  683.4 1.9 fusion.42
  685.4 72.2 %all-gather.14.cloned.1.call-done = bf16[8,8,32,3072]{3,1,0,2:T(8,128)(2,1)} async-done(((bf16[8,8,4,3072]{3,1,0,2:T(8,128)(2,1)}), bf16[8,8,32,3072]{3,1,0,2:T(8,128)(2,1)}) %all-gather.14.cloned.1.call-update) | async-done | bytes 12582928 | tf_op jit(solution)/shard_map/all_gather | solution.py:189
  757.6 14.9 %copy.79 = bf16[8,8,32,3072]{3,2,1,0:T(8,128)(2,1)} copy(bf16[8,8,32,3072]{3,1,0,2:T(8,128)(2,1)} %all-gather.14.cloned.1.call-done) | data formatting | bytes 25165824 | tf_op jit(solution)/shard_map/all_gather | solution.py:189
  772.5 34.3 %fusion.48 = f32[2048,3072]{1,0:T(8,128)} fusion(bf16[768,3072]{1,0:T(8,128)(2,1)} %param.34, bf16[2048,3072]{1,0:T(8,128)(2,1)} %bitcast.148, bf16[3072,768]{1,0:T(8,128)(2,1)} %param.33), kind=kOutput, calls=%fused_computation.56 | convolution fusion | flops 19341508608 | bytes 47185920 | tf_op jit(solution)/shard_map/dot_general | solution.py:199
  806.8 24.8 %copy.80 = f32[8,8,32,3072]{3,1,0,2:T(8,128)} copy(f32[8,8,32,3072]{3,2,1,0:T(8,128)} %bitcast.146) | data formatting | bytes 50331648 | tf_op jit(solution)/shard_map/reshape | solution.py:203
  832.6 10.2 fusion.67
  844.2 144.5 %reduce-scatter.6.cloned.1.call-done = f32[8,8,4,3072]{3,1,0,2:T(8,128)} async-done(((f32[8,8,32,3072]{3,1,0,2:T(8,128)}), f32[8,8,4,3072]{3,1,0,2:T(8,128)}) %reduce-scatter.6.cloned.1.call-update) | async-done | bytes 3145744 | tf_op jit(solution)/shard_map/reduce_scatter | solution.py:204
  988.7 2.5 convert_reduce_fusion.3
  991.8 0.8 fusion.46
  992.6 2.4 copy.84
  995.0 2.8 reshape.400
  997.7 1.6 fusion.111
  999.5 3.5 collective-permute-start
  1003.0 1.3 collective-permute-start.1
  1004.3 80.3 %reduce-scatter.8.cloned.1.call-done = f32[8,16,3072]{2,1,0:T(8,128)} async-done(((f32[8,128,3072]{2,1,0:T(8,128)}), f32[8,16,3072]{2,1,0:T(8,128)}) %reduce-scatter.8.cloned.1.call-update) | async-done | bytes 1572880 | tf_op jit(solution)/shard_map/reduce_scatter | solution.py:185
  1084.6 2.8 add_convert_fusion.1
  1087.4 2.4 copy.86
  (99 shorter events, 9.8 us)
Async XLA Ops:
  7.2 506.6 %copy-start = (bf16[256,3072]{1,0:T(8,128)(2,1)S(1)}, bf16[256,3072]{1,0:T(8,128)(2,1)}, u32[]{:S(2)}) copy-start(bf16[256,3072]{1,0:T(8,128)(2,1)} %param.30) | copy-start | bytes 4718596
  7.2 3.9 copy-start.15
  7.2 4.3 copy-start.16
  7.2 51.0 %all-gather.6.cloned.1.call-start = ((), (), s32[]{:S(2)}) async-start(), calls=%async_computation.3 | async-start | bytes 7077888 | tf_op jit(solution)/shard_map/all_gather | solution.py:107
  7.9 124.9 %all-gather.8.cloned.1.call-start = ((), (), s32[]{:S(2)}) async-start(), calls=%async_computation.4 | async-start | bytes 14155776 | tf_op jit(solution)/shard_map/all_gather | solution.py:106
  11.0 371.0 %all-gather.10.cloned.1.call-start = ((), (), s32[]{:S(2)}) async-start(), calls=%async_computation.5 | async-start | bytes 7864320 | tf_op jit(solution)/shard_map/all_gather | solution.py:154
  24.6 8.1 copy-start.11
  58.2 4.6 copy-start.3
  62.8 2.3 copy-start.6
  70.9 1.6 copy-start.4
  150.5 50.3 %slice-start = ((s8[4718592]{0:T(1024)(128)(4,1)}), s8[524288]{0:T(1024)(128)(4,1)S(1)}, s32[]{:S(2)}) async-start(s8[4718592]{0:T(1024)(128)(4,1)} %bitcast.149), calls=%async_computation.11 | async-start | bytes 1048576
  170.3 30.5 %slice-start.1 = ((s8[4718592]{0:T(1024)(128)(4,1)}), s8[4194304]{0:T(1024)(128)(4,1)S(1)}, s32[]{:S(2)}) async-start(s8[4718592]{0:T(1024)(128)(4,1)} %bitcast.149), calls=%async_computation.12 | async-start | bytes 8388608
  210.8 4.0 copy-start.2
  259.0 6.1 copy-start.9
  266.6 231.1 %all-gather.12.cloned.1.call-start = ((), (), s32[]{:S(2)}) async-start(), calls=%async_computation.6 | async-start | bytes 7864320 | tf_op jit(solution)/shard_map/all_gather | solution.py:155
  268.2 3.3 copy-start.17
  268.2 3.4 copy-start.8
  271.5 408.0 %reduce-scatter.4.cloned.1.call-start = ((), (), s32[]{:S(2)}) async-start(), calls=%async_computation.7 | async-start | bytes 28311552 | tf_op jit(solution)/shard_map/reduce_scatter | solution.py:184
  508.8 1.1 copy-start.7
  524.2 1.0 copy-start.12
  524.2 155.3 %copy-start.5 = (bf16[8,8,4,3072]{3,2,1,0:T(4,128)(2,1)S(1)}, bf16[8,8,4,3072]{3,2,1,0:T(4,128)(2,1)}, u32[]{:S(2)}) copy-start(bf16[8,8,4,3072]{3,2,1,0:T(4,128)(2,1)} %param.18) | copy-start | bytes 4718596
  524.2 233.4 %all-gather.14.cloned.1.call-start = ((), (), s32[]{:S(2)}) async-start(), calls=%async_computation.8 | async-start | bytes 14155776 | tf_op jit(solution)/shard_map/all_gather | solution.py:189
  685.3 303.4 %reduce-scatter.6.cloned.1.call-start = ((), (), s32[]{:S(2)}) async-start(), calls=%async_computation.9 | async-start | bytes 28311552 | tf_op jit(solution)/shard_map/reduce_scatter | solution.py:204
  831.6 1.0 slice-start.2
  831.6 253.0 %reduce-scatter.8.cloned.1.call-start = ((), (), s32[]{:S(2)}) async-start(), calls=%async_computation.10 | async-start | bytes 14155776 | tf_op jit(solution)/shard_map/reduce_scatter | solution.py:185
  842.9 0.7 copy-start.18
  842.9 1.1 copy-start.13
  994.9 4.5 copy-start.14
  994.9 89.7 %copy-start.10 = (f32[8,3072]{1,0:T(8,128)S(1)}, f32[8,3072]{1,0:T(8,128)}, u32[]{:S(2)}) copy-start(f32[8,3072]{1,0:T(8,128)} %get-tuple-element.28) | copy-start | bytes 294916
  999.5 90.3 %collective-permute-start = (f32[8,1,256]{2,1,0:T(1,128)S(1)}, f32[8,1,256]{2,1,0:T(1,128)S(1)}, u32[]{:S(2)}, u32[]{:S(2)}) collective-permute-start(f32[8,1,256]{2,1,0:T(1,128)S(1)} %get-tuple-element.39), channel_id=1, source_target_pairs={{0,8},{8,16},{16,24},{1,9},{9,17},{17,25},{2,10},{10,18},{18,26},{... | collective-permute-start | bytes 24584 | tf_op jit(solution)/shard_map/ppermute | solution.py:24
  1003.0 86.8 %collective-permute-start.1 = (f32[8,1,256]{2,1,0:T(1,128)S(1)}, f32[8,1,256]{2,1,0:T(1,128)S(1)}, u32[]{:S(2)}, u32[]{:S(2)}) collective-permute-start(f32[8,1,256]{2,1,0:T(1,128)S(1)} %get-tuple-element.40), channel_id=1, source_target_pairs={{8,0},{16,8},{24,16},{9,1},{17,9},{25,17},{10,2},{18,10},{26,18},{... | collective-permute-start | bytes 24584 | tf_op jit(solution)/shard_map/ppermute | solution.py:25
  1084.6 5.9 copy-start.1
Sparse Core Ops, SparseCore 0:
  9.9 48.2 all-gather.5
  60.7 72.1 all-gather.7
  266.7 115.3 all-gather.9
  384.1 113.5 all-gather.11
  524.3 155.0 reduce-scatter.3
  685.4 72.1 all-gather.13
  831.7 156.8 reduce-scatter.5
  992.2 92.3 reduce-scatter.7
where the time goes:
time: 1100 us
  waiting for transfers between devices  738 us (67%)
  local copies, waits for them, and re-layouts  124 us (11%)
  other arithmetic  111 us (10%)
  matrix products  104 us (9%)
  between operations  15.1 us (1%)
    reduce_scatter x1, waiting for transfers between devices, per_device(): lax.psum_scatter(image_term, 'tensor', scatter_dimension=2, tiled=True)  154 us
    reduce_scatter x1, waiting for transfers between devices, per_device(): lax.psum_scatter(mlp_term, 'tensor', scatter_dimension=2, tiled=True)  145 us
    all_gather x1, waiting for transfers between devices, per_device(): lax.all_gather(keys, 'tile', axis=1, tiled=True)  110 us
    all_gather x1, waiting for transfers between devices, per_device(): lax.all_gather(values, 'tile', axis=1, tiled=True)  94.9 us
    reduce_scatter x1, waiting for transfers between devices, per_device(): lax.psum_scatter(text_term, 'tensor', scatter_dimension=1, tiled=True)  80.3 us
    all_gather x1, waiting for transfers between devices, per_device(): piece = lax.all_gather(mlp_mod, 'tensor', axis=2, tiled=True)  72.2 us
    all_gather x1, waiting for transfers between devices, per_device(): lax.all_gather(image_hidden, 'tensor', axis=2, tiled=True)  57.5 us
    dot_general x1, matrix products, per_device(): jnp.dot(activated.reshape(requests * image_count, local_units), mlp_reduc...  34.3 us
  transfers between devices with their start and end apart: 10, of which 8 were waited for; matrix products, arithmetic and copies ran while one was open for 9% of the time, Pallas kernels for 0%

commit v1 on v0

v1 whole, which is shorter than its diff:
```python
import math

import jax
import jax.numpy as jnp
from jax import lax
from jax.experimental import pallas as pl
from jax.experimental.pallas import tpu as pltpu
from jax.sharding import PartitionSpec as P

HEAD_DIM = 128
GRID = 32
NSTEPS = 28
CHUNKS = 2


norm_eps = 1e-06
time_shift = 3.0


def padded(value, sides, width):
    for axis, dim in sides:
        size, length = (lax.axis_size(axis), value.shape[dim])
        up = [(i, (i + 1) % size) for i in range(size - 1)]
        down = [(j, i) for i, j in up]
        last = lax.slice_in_dim(value, length - width, length, axis=dim)
        leading = lax.slice_in_dim(value, 0, width, axis=dim)
        before = lax.ppermute(last, axis, up)
        after = lax.ppermute(leading, axis, down)
        value = jnp.concatenate([before, value, after], axis=dim)
    return value


def layer_norm(values):
    average = jnp.mean(values, -1, keepdims=True)
    centred = values - average
    spread = jnp.mean(centred * centred, -1, keepdims=True)
    return centred * lax.rsqrt(spread + norm_eps)


def modulate(hidden, shift, stretch):
    normed = layer_norm(hidden.astype(jnp.float32))
    return ((1.0 + stretch) * normed + shift).astype(jnp.bfloat16)


def rope_tables(row_ids, col_ids):
    pair_index = jnp.arange(64, dtype=jnp.int32)
    row_rank = (pair_index - 8).astype(jnp.float32)
    col_rank = (pair_index - 36).astype(jnp.float32)
    log_base = math.log(10000.0)
    row_freq = jnp.where(
        (pair_index >= 8) & (pair_index < 36), jnp.exp(-2.0 * row_rank / 56.0 * log_base), 0.0
    )
    col_freq = jnp.where(pair_index >= 36, jnp.exp(-2.0 * col_rank / 56.0 * log_base), 0.0)
    angles = row_ids[..., None] * row_freq + col_ids[..., None] * col_freq
    cos_half, sin_half = jnp.cos(angles), jnp.sin(angles)
    return (
        jnp.concatenate([cos_half, cos_half], -1),
        jnp.concatenate([-sin_half, sin_half], -1),
    )


def sigma_of(step_float):
    level = 1.0 - step_float / NSTEPS
    return time_shift * level / (1.0 + (time_shift - 1.0) * level)


def norm_rotate_kernel(heads, image_ref, text_ref, cos_ref, sin_ref, gain_ref, out_ref):
    text_count = text_ref.shape[2]
    image_count = image_ref.shape[2]

    def head_norm(values, gain):
        squares = jnp.mean(values * values, -1, keepdims=True)
        return values * lax.rsqrt(squares + norm_eps) * gain

    for r in range(image_ref.shape[1]):
        cos_table = cos_ref[0, r]
        sin_table = sin_ref[0, r]
        for kind in range(3):
            for h in range(heads):
                at = (kind * heads + h) * HEAD_DIM
                image = image_ref[0, r, :, at : at + HEAD_DIM]
                text = text_ref[0, r, :, at : at + HEAD_DIM]
                if kind < 2:
                    image = head_norm(image, gain_ref[kind : kind + 1, :])
                    text = head_norm(text, gain_ref[2 + kind : 3 + kind, :])
                    image = image * cos_table + pltpu.roll(image, HEAD_DIM // 2, 1) * sin_table
                out_ref[r, kind, h, 0, :text_count, :] = text.astype(jnp.bfloat16)
                out_ref[r, kind, h, 0, text_count : text_count + image_count, :] = image.astype(
                    jnp.bfloat16
                )


def norm_rotate(image_qkv, text_qkv, cos_table, sin_table, gains, heads):
    parts, requests, image_count, width = image_qkv.shape
    text_count = text_qkv.shape[2]
    count = image_count + text_count

    def rows(n, w):
        return pl.BlockSpec((1, requests, n, w), lambda i: (i, 0, 0, 0))

    return pl.pallas_call(
        lambda *refs: norm_rotate_kernel(heads, *refs),
        grid=(parts,),
        out_shape=jax.ShapeDtypeStruct(
            (requests, 3, heads, parts, count, HEAD_DIM), jnp.bfloat16
        ),
        in_specs=[
            rows(image_count, width),
            rows(text_count, width),
            rows(image_count, HEAD_DIM),
            rows(image_count, HEAD_DIM),
            pl.BlockSpec((4, HEAD_DIM), lambda i: (0, 0)),
        ],
        out_specs=pl.BlockSpec(
            (requests, 3, heads, 1, count, HEAD_DIM), lambda i: (0, 0, 0, i, 0, 0)
        ),
        compiler_params=pltpu.CompilerParams(vmem_limit_bytes=32 * 1024 * 1024),
        cost_estimate=pl.CostEstimate(
            flops=12 * parts * requests * count * width,
            bytes_accessed=6 * parts * requests * count * width,
            transcendentals=0,
        ),
    )(image_qkv, text_qkv, cos_table, sin_table, gains)


def split_pairs(weight, heads):
    width, _, cols = weight.shape
    place = jnp.arange(HEAD_DIM, dtype=jnp.int32)
    source = (place % (HEAD_DIM // 2)) * 2 + place // (HEAD_DIM // 2)
    one_head = (place[:, None] == source[None, :]).astype(jnp.bfloat16)
    block = jnp.kron(jnp.eye(2 * heads, dtype=jnp.bfloat16), one_head)
    flat = weight.reshape(width, 3 * cols)
    moved = jnp.dot(flat[:, : 2 * cols], block, preferred_element_type=jnp.float32)
    return jnp.concatenate([moved.astype(jnp.bfloat16), flat[:, 2 * cols :]], 1)


def rotated_pairs(size, step):
    return [(i, (i + step) % size) for i in range(size)]


def attend(query, keys, values, owners, text_len, text_count, part_count, tile_text):
    offset = jnp.arange(keys.shape[2] // len(owners), dtype=jnp.int32)
    part, inner = offset // part_count, offset % part_count
    local = jnp.where(inner < text_count, part * text_count + inner, -1)
    text_pos = jnp.concatenate(
        [jnp.where(local < 0, -1, owner * tile_text + local) for owner in owners]
    )
    usable = (text_pos[None, :] < text_len[:, None])[:, None, None, :]
    score_scale = 1.0 / math.sqrt(HEAD_DIM)
    scores = (
        jnp.einsum("rhqd,rhkd->rhqk", query, keys, preferred_element_type=jnp.float32)
        * score_scale
    )
    row_top = jnp.max(jnp.where(usable, scores, -jnp.inf), -1, keepdims=True)
    weights = jnp.where(usable, jnp.exp(scores - row_top), 0.0)
    weight_sum = jnp.sum(weights, -1, keepdims=True)
    accum = jnp.einsum(
        "rhqk,rhkd->rhqd",
        weights.astype(jnp.bfloat16),
        values,
        preferred_element_type=jnp.float32,
    )
    return (accum / weight_sum).astype(jnp.bfloat16)


def per_device(
    image_hidden,
    text_hidden,
    latents,
    step_index,
    anchor,
    text_len,
    mod_image,
    mod_text,
    mod_mlp,
    mod_final,
    qkv_image,
    qkv_text,
    proj_image,
    proj_text,
    qk_gain,
    mlp_expand,
    mlp_reduce,
    final_weight,
):
    all_requests, tile_rows, tile_cols, model_width = image_hidden.shape
    local_cols = qkv_image.shape[2]
    heads = local_cols // HEAD_DIM
    local_units = mlp_expand.shape[1]
    tiles = lax.axis_size("tile")
    parts = lax.axis_size("tensor")
    tile_index = lax.axis_index("tile")
    text_count = text_hidden.shape[1]
    image_count = tile_rows * tile_cols
    part_count = text_count + image_count
    by_request = all_requests % tiles == 0
    chunks = CHUNKS if all_requests % (CHUNKS * tiles) == 0 else 1
    requests = all_requests // chunks
    own = requests // tiles

    image_w = split_pairs(qkv_image, heads)
    text_w = split_pairs(qkv_text, heads)
    gains = qk_gain.reshape(4, HEAD_DIM // 2, 2).transpose(0, 2, 1).reshape(4, HEAD_DIM)
    part_index = jnp.arange(parts, dtype=jnp.int32)[:, None, None]
    token = jnp.arange(image_count, dtype=jnp.int32)[None, None, :]
    row_ids = anchor[None, :, 0:1] + tile_index * tile_rows + token // tile_cols + 0 * part_index
    col_ids = anchor[None, :, 1:2] + part_index * tile_cols + token % tile_cols
    cos_table, sin_table = rope_tables(row_ids.astype(jnp.float32), col_ids.astype(jnp.float32))
    step_float = step_index.astype(jnp.float32)
    time_delta = sigma_of(step_float + 1.0) - sigma_of(step_float)

    def rows_of(value, c):
        return value[c * requests : (c + 1) * requests]

    def gather(value):
        return lax.all_gather(value, "tensor", axis=0, tiled=False)

    def scatter(value):
        return lax.psum_scatter(value, "tensor", scatter_dimension=0, tiled=False)

    def exchange_attend(joint, lengths):
        blocks, owners = [], []
        for step in range(tiles):
            to = lax.rem(tile_index + step, tiles)
            block = lax.dynamic_slice_in_dim(joint, to * own, own, 0)
            if step:
                block = lax.ppermute(block, "tile", rotated_pairs(tiles, step))
            blocks.append(block)
            owners.append(lax.rem(tile_index + tiles - step, tiles))
        whole = jnp.concatenate(blocks, 3)
        attended = attend(
            whole[:, 0],
            whole[:, 1],
            whole[:, 2],
            owners,
            lax.dynamic_slice_in_dim(lengths, tile_index * own, own, 0),
            text_count,
            part_count,
            text_count * parts,
        )
        count = parts * part_count
        back = []
        for step in range(tiles):
            block = attended[:, :, step * count : (step + 1) * count]
            if step:
                block = lax.ppermute(block, "tile", rotated_pairs(tiles, tiles - step))
            back.append(block)
        return lax.dynamic_slice_in_dim(
            jnp.concatenate(back + back, 0),
            lax.rem(tiles - tile_index, tiles) * own,
            requests,
            0,
        )

    hidden, text, gathered = [], [], []
    for c in range(chunks):
        image_c = rows_of(image_hidden, c).reshape(requests, image_count, model_width)
        text_c = rows_of(text_hidden, c)
        mi, mt = rows_of(mod_image, c), rows_of(mod_text, c)
        hidden.append(image_c)
        text.append(text_c)
        gathered.append(
            (
                gather(modulate(text_c, mt[:, 0, None, :], mt[:, 1, None, :])),
                gather(modulate(image_c, mi[:, 0, None, :], mi[:, 1, None, :])),
            )
        )

    image_sums, text_sums = [], []
    for c in range(chunks):
        text_mod, image_mod = gathered[c]
        text_qkv = jnp.dot(
            text_mod.reshape(-1, model_width), text_w, preferred_element_type=jnp.float32
        ).reshape(parts, requests, text_count, 3 * local_cols)
        image_qkv = jnp.dot(
            image_mod.reshape(-1, model_width), image_w, preferred_element_type=jnp.float32
        ).reshape(parts, requests, image_count, 3 * local_cols)
        in_chunk = slice(c * requests, (c + 1) * requests)
        joint = norm_rotate(
            image_qkv, text_qkv, cos_table[:, in_chunk], sin_table[:, in_chunk], gains, heads
        ).reshape(requests, 3, heads, parts * part_count, HEAD_DIM)
        if by_request:
            attended = exchange_attend(joint, rows_of(text_len, c))
        else:
            every = lax.all_gather(joint[:, 1:], "tile", axis=3, tiled=True)
            attended = attend(
                joint[:, 0],
                every[:, 0],
                every[:, 1],
                list(range(tiles)),
                rows_of(text_len, c),
                text_count,
                part_count,
                text_count * parts,
            )
        ordered = attended.reshape(requests, heads, parts, part_count, HEAD_DIM)
        ordered = ordered.transpose(2, 0, 3, 1, 4).reshape(parts, requests, part_count, local_cols)
        image_term = jnp.dot(
            ordered[:, :, text_count:].reshape(-1, local_cols),
            proj_image,
            preferred_element_type=jnp.float32,
        ).astype(jnp.bfloat16)
        image_sums.append(scatter(image_term.reshape(parts, requests, image_count, model_width)))
        text_sums.append((ordered, c))

    mids, mods = [], []
    for c in range(chunks):
        gate = rows_of(mod_image, c)[:, 2, None, :]
        mm = rows_of(mod_mlp, c)
        image_mid = (
            hidden[c].astype(jnp.float32) + gate * image_sums[c].astype(jnp.float32)
        ).astype(jnp.bfloat16)
        mids.append(image_mid)
        mods.append(gather(modulate(image_mid, mm[:, 0, None, :], mm[:, 1, None, :])))

    image_outs, text_outs, nexts = [], [], []
    for c in range(chunks):
        mm = rows_of(mod_mlp, c)
        mf = rows_of(mod_final, c)
        ordered, _ = text_sums[c]
        text_term = jnp.dot(
            ordered[:, :, :text_count].reshape(-1, local_cols),
            proj_text,
            preferred_element_type=jnp.float32,
        ).astype(jnp.bfloat16)
        text_sum = scatter(text_term.reshape(parts, requests, text_count, model_width))
        text_outs.append(
            (
                text[c].astype(jnp.float32)
                + rows_of(mod_text, c)[:, 2, None, :] * text_sum.astype(jnp.float32)
            ).astype(jnp.bfloat16)
        )
        grown = jnp.dot(
            mods[c].reshape(-1, model_width), mlp_expand, preferred_element_type=jnp.float32
        )
        activated = jax.nn.gelu(grown, approximate=True).astype(jnp.bfloat16)
        mlp_term = jnp.dot(activated, mlp_reduce, preferred_element_type=jnp.float32).astype(
            jnp.bfloat16
        )
        mlp_sum = scatter(mlp_term.reshape(parts, requests, image_count, model_width))
        image_out = (
            mids[c].astype(jnp.float32) + mm[:, 2, None, :] * mlp_sum.astype(jnp.float32)
        ).astype(jnp.bfloat16)
        image_outs.append(image_out)
        final_in = modulate(image_out, mf[:, 0, None, :], mf[:, 1, None, :])
        velocity = jnp.dot(
            final_in.reshape(-1, model_width), final_weight, preferred_element_type=jnp.float32
        ).reshape(requests, tile_rows, tile_cols * final_weight.shape[1])
        nexts.append(rows_of(latents, c) + rows_of(time_delta, c)[:, None, None] * velocity)

    image_out = jnp.concatenate(image_outs, 0).reshape(image_hidden.shape)
    text_out = jnp.concatenate(text_outs, 0)
    latents_ext = padded(jnp.concatenate(nexts, 0), (("tile", 1),), 1)
    return (image_out, text_out, latents_ext)


def solution(mesh):
    return jax.shard_map(
        per_device,
        mesh=mesh,
        in_specs=(
            P(None, "tile", "tensor", None),
            P(None, ("tile", "tensor"), None),
            P(None, "tile", "tensor"),
            P(),
            P(),
            P(),
            P(),
            P(),
            P(),
            P(),
            P(None, None, "tensor"),
            P(None, None, "tensor"),
            P("tensor", None),
            P("tensor", None),
            P(),
            P(None, "tensor"),
            P("tensor", None),
            P(),
        ),
        out_specs=(
            P(None, "tile", "tensor", None),
            P(None, ("tile", "tensor"), None),
            P(None, "tile", "tensor"),
        ),
        check_vma=False,
    )
```

time: 1100 us -> 785 us (0.71)
  waiting for transfers between devices: 738 us -> 436 us
  local copies, waits for them, and re-layouts: 124 us -> 64.9 us
  other arithmetic: 111 us -> 61.1 us
  starting transfers between devices: 5.34 us -> 44 us
  matrix products: 104 us -> 137 us
  Pallas kernels: 0 us -> 21.1 us
    all_gather x5 -> x6, waiting for transfers between devices: 359 us -> 84 us  [gather(): return lax.all_gather(value, 'tensor', axis=0, tiled=False)]
    reduce_scatter x3 -> x6, waiting for transfers between devices: 379 us -> 245 us  [scatter(): return lax.psum_scatter(value, 'tensor', scatter_dimension=0, tiled=False)]
    ppermute x0 -> x12, waiting for transfers between devices: none -> 105 us  [the longest x6 72.2 us: exchange_attend(): block = lax.ppermute(block, 'tile', rotated_pairs(tiles, step))]
    ppermute x0 -> x12, starting transfers between devices: none -> 38 us  [the longest x6 28.6 us: exchange_attend(): block = lax.ppermute(block, 'tile', rotated_pairs(tiles, tiles - step))]
    dot_general x7 -> x16, matrix products: 83.3 us -> 114 us  [the longest x2 38.9 us: per_device(): jnp.dot(activated, mlp_reduce, preferred_element_type=jnp.float32)]
    reshape x5 -> x6, local copies, waits for them, and re-layouts: 35 us -> 4.77 us  [the longest x2 2.94 us: per_device(): ordered.transpose(2, 0, 3, 1, 4)]
    rev x2 -> x0, local copies, waits for them, and re-layouts: 21.8 us -> none  [rotate(): swapped = jnp.flip(paired, -1).reshape(values.shape)]
    pallas_call x0 -> x2, Pallas kernels: none -> 21.1 us  [norm_rotate(): pl.pallas_call(lambda *refs: norm_rotate_kernel(heads, *refs), grid=(part...]
  transfers between devices with their start and end apart: 10 -> 26, of which waited for: 8 -> 17; matrix products, arithmetic and copies ran while one was open for 9% -> 29% of each run, Pallas kernels for 0% -> 3%
where the time goes in v1:
time: 785 us; the launch traced here: 779 us
  waiting for transfers between devices  436 us (56%)
  matrix products  137 us (17%)
  local copies, waits for them, and re-layouts  64.9 us (8%)
  other arithmetic  61.1 us (8%)
  starting transfers between devices  44 us (6%)
  Pallas kernels  21.1 us (3%)
  between operations  15.2 us (2%)
    reduce_scatter x6, waiting for transfers between devices, scatter(): return lax.psum_scatter(value, 'tensor', scatter_dimension=0, tiled=False)  245 us
    all_gather x6, waiting for transfers between devices, gather(): return lax.all_gather(value, 'tensor', axis=0, tiled=False)  84 us
    ppermute x6, waiting for transfers between devices, exchange_attend(): block = lax.ppermute(block, 'tile', rotated_pairs(tiles, step))  72.2 us
    dot_general x2, matrix products, per_device(): jnp.dot(activated, mlp_reduce, preferred_element_type=jnp.float32)  38.9 us
    ppermute x6, waiting for transfers between devices, exchange_attend(): block = lax.ppermute(block, 'tile', rotated_pairs(tiles, tiles - step))  32.4 us
    ppermute x6, starting transfers between devices, exchange_attend(): block = lax.ppermute(block, 'tile', rotated_pairs(tiles, tiles - step))  28.6 us
    unnamed x96, local copies, waits for them, and re-layouts  26.6 us
    sub x2, matrix products, attend(): weights = jnp.where(usable, jnp.exp(scores - row_top), 0.0)  22.4 us
  transfers between devices with their start and end apart: 26, of which 17 were waited for; matrix products, arithmetic and copies ran while one was open for 29% of the time, Pallas kernels for 3%

profile of v1, /device:TPU:0, one launch (start us, length us, event | category | flops | bytes accessed | tf_op | source)
XLA Modules:
  0.0 779.3 jit_solution(1797078832524312316)
XLA Ops:
  15.8 2.1 slice_convert_fusion.1
  17.9 2.8 reshape.813
  20.7 2.8 add_convert_fusion.3
  26.3 2.6 add_convert_fusion.7
  29.2 6.7 copy.80
  35.9 2.7 slice.287
  38.5 6.7 copy.77
  45.2 2.7 slice.285
  48.6 3.8 fusion.120
  54.1 5.6 fusion.21
  59.8 3.5 fusion.20
  63.3 7.1 fusion.40.refs_1_
  70.4 24.6 %all-gather.13.cloned.1.call-done = bf16[8,4,32,3072]{3,2,1,0:T(8,128)(2,1)} async-done(((bf16[1,4,32,3072]{3,2,1,0:T(8,128)(2,1)}), bf16[8,4,32,3072]{3,2,1,0:T(8,128)(2,1)}) %all-gather.13.cloned.1.call-update) | async-done | bytes 6291472 | tf_op jit(solution)/shard_map/all_gather | solution.py:216
  95.1 9.0 %fusion.42.refs_0_ = f32[8,4,32,768]{3,2,1,0:T(8,128)S(1)} fusion(bf16[8,4,32,3072]{3,2,1,0:T(8,128)(2,1)} %all-gather.13.cloned.1.call-done, bf16[3072,256]{0,1:T(8,128)(2,1)} %slice.285, bf16[3072,512]{0,1:T(8,128)(2,1)} %fusion.20), kind=kOutput, calls=%fused_computation.54 | convolution fusion | flops 4841275392 | bytes 14155776 | tf_op jit(solution)/shard_map/dot_general | solution.py:275
  104.0 10.6 %shard_map.194 = bf16[4,3,2,8,48,128]{5,4,3,2,1,0:T(8,128)(2,1)S(1)} custom-call(f32[8,4,32,768]{3,2,1,0:T(8,128)S(1)} %fusion.42.refs_0_, f32[8,4,16,768]{3,2,1,0:T(8,128)S(1)} %copy-done.3, f32[8,4,32,128]{3,2,1,0:T(8,128)S(1)} %get-tuple-element.43.refs_2_, f32[8,4,32,128]{3,2,1,0:T(8,128)S(1)} %copy-done.1, f32[4,128]{1,0:T(4,128)S(1)} %reshape.783.refs_4_), custom_call_target="tpu_custom_call" | custom-call | flops 14155776 | bytes 7077888 | tf_op jit(solution)/shard_map/pallas_call | solution.py:101
  116.4 2.4 collective-permute-start.7
  122.8 10.2 %collective-permute-done.6 = bf16[1,3,2,384,128]{4,3,2,1,0:T(8,128)(2,1)S(1)} collective-permute-done((bf16[1,3,2,384,128]{4,3,2,1,0:T(8,128)(2,1)S(1)}, bf16[1,3,2,384,128]{4,3,2,1,0:T(8,128)(2,1)S(1)}, u32[]{:S(2)}, u32[]{:S(2)}) %collective-permute-start.6) | collective-permute-done | bytes 589856 | tf_op jit(solution)/shard_map/ppermute | solution.py:227
  133.0 24.6 %collective-permute-done.7 = bf16[1,3,2,384,128]{4,3,2,1,0:T(8,128)(2,1)S(1)} collective-permute-done((bf16[1,3,2,384,128]{4,3,2,1,0:T(8,128)(2,1)S(1)}, bf16[1,3,2,384,128]{4,3,2,1,0:T(8,128)(2,1)S(1)}, u32[]{:S(2)}, u32[]{:S(2)}) %collective-permute-start.7) | collective-permute-done | bytes 589856 | tf_op jit(solution)/shard_map/ppermute | solution.py:227
  159.1 11.2 %fusion.166 = (f32[2,1536]{1,0:T(2,128)S(1)}, bf16[2,1536,1536]{1,2,0:T(8,128)(2,1)}) fusion(pred[1536]{0:T(1024)(128)(4,1)S(1)} %get-tuple-element.86, bf16[1,3,2,1536,128]{4,3,2,1,0:T(8,128)(2,1)} %pad_maximum_fusion.1), kind=kOutput, calls=%fused_computation.328 | convolution fusion | flops 2448950784 | bytes 12599296 | tf_op jit(solution)/shard_map/sub | solution.py:155
  170.3 7.8 fusion.56
  179.0 13.9 %collective-permute-start.9 = (bf16[1,2,384,128]{3,2,1,0:T(8,128)(2,1)}, bf16[1,2,384,128]{3,2,1,0:T(8,128)(2,1)}, u32[]{:S(2)}, u32[]{:S(2)}) collective-permute-start(bf16[1,2,384,128]{3,2,1,0:T(8,128)(2,1)} %get-tuple-element.55), channel_id=1, source_target_pairs={{0,24},{8,0},{16,8},{24,16},{1,25},{9,1},{17,9},{25,17},{2,26},{10... | collective-permute-start | bytes 589832 | tf_op jit(solution)/shard_map/ppermute | solution.py:246
  193.9 4.8 collective-permute-done.9
  200.2 11.1 %collective-permute-done.10 = bf16[1,2,384,128]{3,2,1,0:T(8,128)(2,1)} collective-permute-done((bf16[1,2,384,128]{3,2,1,0:T(8,128)(2,1)}, bf16[1,2,384,128]{3,2,1,0:T(8,128)(2,1)}, u32[]{:S(2)}, u32[]{:S(2)}) %collective-permute-start.10) | collective-permute-done | bytes 196640 | tf_op jit(solution)/shard_map/ppermute | solution.py:246
  221.2 2.4 reshape.799
  223.7 4.5 convolution_convert_fusion.1
  228.3 7.7 fusion.41.refs_1_
  235.9 9.9 %fusion.43.refs_0_ = f32[8,4,32,768]{3,2,1,0:T(8,128)S(1)} fusion(bf16[8,4,32,3072]{3,2,1,0:T(8,128)(2,1)} %all-gather.9.cloned.1.call-done, bf16[3072,256]{0,1:T(8,128)(2,1)} %slice.285, bf16[3072,512]{0,1:T(8,128)(2,1)} %fusion.20), kind=kOutput, calls=%fused_computation.55 | convolution fusion | flops 4841275392 | bytes 14155776 | tf_op jit(solution)/shard_map/dot_general | solution.py:275
  245.8 10.6 %shard_map.193 = bf16[4,3,2,8,48,128]{5,4,3,2,1,0:T(8,128)(2,1)S(1)} custom-call(f32[8,4,32,768]{3,2,1,0:T(8,128)S(1)} %fusion.43.refs_0_, f32[8,4,16,768]{3,2,1,0:T(8,128)S(1)} %copy-done.2, f32[8,4,32,128]{3,2,1,0:T(8,128)S(1)} %get-tuple-element.42.refs_2_, f32[8,4,32,128]{3,2,1,0:T(8,128)S(1)} %get-tuple-element.36.refs_3_, f32[4,128]{1,0:T(4,128)S(1)} %reshape.783.refs_4_), custom_call_target="tpu_custom_call" | custom-call | flops 14155776 | bytes 7077888 | tf_op jit(solution)/shard_map/pallas_call | solution.py:101
  256.7 3.9 collective-permute-start.2
  260.6 14.2 %collective-permute-done = bf16[1,3,2,384,128]{4,3,2,1,0:T(8,128)(2,1)S(1)} collective-permute-done((bf16[1,3,2,384,128]{4,3,2,1,0:T(8,128)(2,1)S(1)}, bf16[1,3,2,384,128]{4,3,2,1,0:T(8,128)(2,1)S(1)}, u32[]{:S(2)}, u32[]{:S(2)}) %collective-permute-start) | collective-permute-done | bytes 589856 | tf_op jit(solution)/shard_map/ppermute | solution.py:227
  274.8 23.2 %collective-permute-done.1 = bf16[1,3,2,384,128]{4,3,2,1,0:T(8,128)(2,1)S(1)} collective-permute-done((bf16[1,3,2,384,128]{4,3,2,1,0:T(8,128)(2,1)S(1)}, bf16[1,3,2,384,128]{4,3,2,1,0:T(8,128)(2,1)S(1)}, u32[]{:S(2)}, u32[]{:S(2)}) %collective-permute-start.1) | collective-permute-done | bytes 589856 | tf_op jit(solution)/shard_map/ppermute | solution.py:227
  299.5 11.3 %fusion.165 = (f32[2,1536]{1,0:T(2,128)S(1)}, bf16[2,1536,1536]{1,2,0:T(8,128)(2,1)}) fusion(pred[1536]{0:T(1024)(128)(4,1)S(1)} %get-tuple-element.85, bf16[1,3,2,1536,128]{4,3,2,1,0:T(8,128)(2,1)} %pad_maximum_fusion), kind=kOutput, calls=%fused_computation.327 | convolution fusion | flops 2448950784 | bytes 12599296 | tf_op jit(solution)/shard_map/sub | solution.py:155
  310.8 7.7 fusion.59
  318.5 10.9 %collective-permute-start.3 = (bf16[1,2,384,128]{3,2,1,0:T(8,128)(2,1)S(1)}, bf16[1,2,384,128]{3,2,1,0:T(8,128)(2,1)S(1)}, u32[]{:S(2)}, u32[]{:S(2)}) collective-permute-start(bf16[1,2,384,128]{3,2,1,0:T(8,128)(2,1)S(1)} %get-tuple-element.49), channel_id=1, source_target_pairs={{0,24},{8,0},{16,8},{24,16},{1,25},{9,1},{17,9},{25,17},{2,26},{10... | collective-permute-start | bytes 589832 | tf_op jit(solution)/shard_map/ppermute | solution.py:246
  329.4 2.9 collective-permute-start.4
  332.3 2.7 collective-permute-done.3
  335.0 13.8 %collective-permute-done.4 = bf16[1,2,384,128]{3,2,1,0:T(8,128)(2,1)S(1)} collective-permute-done((bf16[1,2,384,128]{3,2,1,0:T(8,128)(2,1)S(1)}, bf16[1,2,384,128]{3,2,1,0:T(8,128)(2,1)S(1)}, u32[]{:S(2)}, u32[]{:S(2)}) %collective-permute-start.4) | collective-permute-done | bytes 196640 | tf_op jit(solution)/shard_map/ppermute | solution.py:246
  350.5 4.5 convolution_convert_fusion.3
  356.7 2.7 reshape.814
  359.5 54.7 %reduce-scatter.7.cloned.1.call-done = bf16[1,4,32,3072]{3,2,1,0:T(8,128)(2,1)} async-done(((bf16[8,4,32,3072]{3,2,1,0:T(8,128)(2,1)}), bf16[1,4,32,3072]{3,2,1,0:T(8,128)(2,1)}) %reduce-scatter.7.cloned.1.call-update) | async-done | bytes 786448 | tf_op jit(solution)/shard_map/reduce_scatter | solution.py:219
  414.2 2.6 reshape.811
  416.8 4.7 convert_reduce_fusion.1
  423.5 2.9 add_convert_fusion
  429.2 2.6 add_convert_fusion.4
  431.8 4.2 convolution_convert_fusion.4
  437.4 2.7 convolution_convert_fusion.5
  440.2 31.9 %all-gather.15.cloned.1.call-done = bf16[8,4,32,3072]{3,2,1,0:T(8,128)(2,1)} async-done(((bf16[1,4,32,3072]{3,2,1,0:T(8,128)(2,1)}), bf16[8,4,32,3072]{3,2,1,0:T(8,128)(2,1)}) %all-gather.15.cloned.1.call-update) | async-done | bytes 6291472 | tf_op jit(solution)/shard_map/all_gather | solution.py:216
  472.1 19.5 %convolution_convert_fusion = bf16[1024,3072]{1,0:T(8,128)(2,1)} fusion(bf16[768,3072]{1,0:T(8,128)(2,1)} %param.34, bf16[1024,3072]{1,0:T(8,128)(2,1)} %bitcast.307, bf16[3072,768]{1,0:T(8,128)(2,1)} %param.33), kind=kOutput, calls=%fused_computation.20 | convolution fusion | flops 9673900032 | bytes 22020096 | tf_op jit(solution)/shard_map/dot_general | solution.py:337
  492.0 27.5 %all-gather.11.cloned.1.call-done = bf16[8,4,32,3072]{3,2,1,0:T(8,128)(2,1)} async-done(((bf16[1,4,32,3072]{3,2,1,0:T(8,128)(2,1)}), bf16[8,4,32,3072]{3,2,1,0:T(8,128)(2,1)}) %all-gather.11.cloned.1.call-update) | async-done | bytes 6291472 | tf_op jit(solution)/shard_map/all_gather | solution.py:216
  519.5 19.4 %convolution_convert_fusion.2 = bf16[1024,3072]{1,0:T(8,128)(2,1)} fusion(bf16[768,3072]{1,0:T(8,128)(2,1)} %param.34, bf16[1024,3072]{1,0:T(8,128)(2,1)} %bitcast.308, bf16[3072,768]{1,0:T(8,128)(2,1)} %param.33), kind=kOutput, calls=%fused_computation.22 | convolution fusion | flops 9673900032 | bytes 22020096 | tf_op jit(solution)/shard_map/dot_general | solution.py:337
  539.0 2.9 reshape.821
  545.2 24.0 %reduce-scatter.17.cloned.1.call-done = bf16[1,4,16,3072]{3,2,1,0:T(8,128)(2,1)} async-done(((bf16[8,4,16,3072]{3,2,1,0:T(8,128)(2,1)}), bf16[1,4,16,3072]{3,2,1,0:T(8,128)(2,1)}) %reduce-scatter.17.cloned.1.call-update) | async-done | bytes 393232 | tf_op jit(solution)/shard_map/reduce_scatter | solution.py:219
  569.2 49.9 %reduce-scatter.15.cloned.1.call-done = bf16[1,4,16,3072]{3,2,1,0:T(8,128)(2,1)} async-done(((bf16[8,4,16,3072]{3,2,1,0:T(8,128)(2,1)}), bf16[1,4,16,3072]{3,2,1,0:T(8,128)(2,1)}) %reduce-scatter.15.cloned.1.call-update) | async-done | bytes 393232 | tf_op jit(solution)/shard_map/reduce_scatter | solution.py:219
  621.7 62.6 %reduce-scatter.13.cloned.1.call-done = bf16[1,4,32,3072]{3,2,1,0:T(8,128)(2,1)} async-done(((bf16[8,4,32,3072]{3,2,1,0:T(8,128)(2,1)}), bf16[1,4,32,3072]{3,2,1,0:T(8,128)(2,1)}) %reduce-scatter.13.cloned.1.call-update) | async-done | bytes 786448 | tf_op jit(solution)/shard_map/reduce_scatter | solution.py:219
  684.2 2.6 reshape.815
  686.8 3.2 convert_reduce_fusion.2
  692.1 2.8 fusion.78
  696.0 53.6 %reduce-scatter.9.cloned.1.call-done = bf16[1,4,32,3072]{3,2,1,0:T(8,128)(2,1)} async-done(((bf16[8,4,32,3072]{3,2,1,0:T(8,128)(2,1)}), bf16[1,4,32,3072]{3,2,1,0:T(8,128)(2,1)}) %reduce-scatter.9.cloned.1.call-update) | async-done | bytes 786448 | tf_op jit(solution)/shard_map/reduce_scatter | solution.py:219
  749.6 2.7 reshape.812
  752.4 3.1 convert_reduce_fusion.3
  757.6 2.3 fusion.83
  762.7 3.4 collective-permute-start.12
  767.4 2.2 pad_maximum_fusion.2
  769.5 2.1 collective-permute-done.13
  (230 shorter events, 62.2 us)
Async XLA Ops:
  7.2 216.5 %copy-start = (bf16[256,3072]{1,0:T(8,128)(2,1)S(1)}, bf16[256,3072]{1,0:T(8,128)(2,1)}, u32[]{:S(2)}) copy-start(bf16[256,3072]{1,0:T(8,128)(2,1)} %param.30) | copy-start | bytes 4718596
  7.2 56.1 %all-gather.19.cloned.1.call-start = ((), (), s32[]{:S(2)}) async-start(), calls=%async_computation.17 | async-start | bytes 3538944 | tf_op jit(solution)/shard_map/all_gather | solution.py:216
  7.2 3.4 copy-start.9
  10.6 1.9 copy-start.4
  12.4 82.6 %all-gather.13.cloned.1.call-start = ((), (), s32[]{:S(2)}) async-start(), calls=%async_computation.10 | async-start | bytes 7077888 | tf_op jit(solution)/shard_map/all_gather | solution.py:216
  15.7 407.7 %copy-start.21 = (f32[4,3072]{1,0:T(4,128)}, f32[4,3072]{1,0:T(4,128)S(1)}, u32[]{:S(2)}) copy-start(f32[4,3072]{1,0:T(4,128)S(1)} %get-tuple-element.73) | copy-start | bytes 147460
  15.7 413.4 %copy-start.20 = (f32[4,3072]{1,0:T(4,128)}, f32[4,3072]{1,0:T(4,128)S(1)}, u32[]{:S(2)}) copy-start(f32[4,3072]{1,0:T(4,128)S(1)} %get-tuple-element.68) | copy-start | bytes 147460
  20.7 3.9 copy-start.6
  23.6 204.7 %all-gather.17.cloned.1.call-start = ((), (), s32[]{:S(2)}) async-start(), calls=%async_computation.16 | async-start | bytes 3538944 | tf_op jit(solution)/shard_map/all_gather | solution.py:216
  24.3 211.6 %all-gather.9.cloned.1.call-start = ((), (), s32[]{:S(2)}) async-start(), calls=%async_computation.6 | async-start | bytes 7077888 | tf_op jit(solution)/shard_map/all_gather | solution.py:216
  28.9 327.8 %reduce-scatter.11.cloned.1.call-start = ((), (), s32[]{:S(2)}) async-start(), calls=%async_computation.11 | async-start | bytes 7077888 | tf_op jit(solution)/shard_map/reduce_scatter | solution.py:219
  45.2 2.8 copy-start.28
  45.2 3.1 copy-start.30
  53.8 5.9 slice-start
  54.1 5.7 slice-start.1
  95.0 9.0 %copy-start.1 = (f32[8,4,32,128]{3,2,1,0:T(8,128)S(1)}, f32[8,4,32,128]{3,2,1,0:T(8,128)}, u32[]{:S(2)}) copy-start(f32[8,4,32,128]{3,2,1,0:T(8,128)} %get-tuple-element.37.refs_3_) | copy-start | bytes 1572868
  95.1 9.0 %copy-start.3 = (f32[8,4,16,768]{3,2,1,0:T(8,128)S(1)}, f32[8,4,16,768]{3,2,1,0:T(8,128)}, u32[]{:S(2)}) copy-start(f32[8,4,16,768]{3,2,1,0:T(8,128)} %fusion.40.refs_1_) | copy-start | bytes 4718596
  114.6 5.6 copy-start.29
  114.8 18.2 %collective-permute-start.6 = (bf16[1,3,2,384,128]{4,3,2,1,0:T(8,128)(2,1)S(1)}, bf16[1,3,2,384,128]{4,3,2,1,0:T(8,128)(2,1)S(1)}, u32[]{:S(2)}, u32[]{:S(2)}) collective-permute-start(bf16[1,3,2,384,128]{4,3,2,1,0:T(8,128)(2,1)S(1)} %get-tuple-element.35), channel_id=1, source_target_pairs={{0,8},{8,16},{16,24},{24,0},{1,9},{9,17},{17,25},{25,1},{2,10},{10... | collective-permute-start | bytes 1769480 | tf_op jit(solution)/shard_map/ppermute | solution.py:227
  116.4 41.2 %collective-permute-start.7 = (bf16[1,3,2,384,128]{4,3,2,1,0:T(8,128)(2,1)S(1)}, bf16[1,3,2,384,128]{4,3,2,1,0:T(8,128)(2,1)S(1)}, u32[]{:S(2)}, u32[]{:S(2)}) collective-permute-start(bf16[1,3,2,384,128]{4,3,2,1,0:T(8,128)(2,1)S(1)} %get-tuple-element.34), channel_id=1, source_target_pairs={{0,16},{8,24},{16,0},{24,8},{1,17},{9,25},{17,1},{25,9},{2,18},{10... | collective-permute-start | bytes 1769480 | tf_op jit(solution)/shard_map/ppermute | solution.py:227
  118.8 38.8 %collective-permute-start.8 = (bf16[1,3,2,384,128]{4,3,2,1,0:T(8,128)(2,1)S(1)}, bf16[1,3,2,384,128]{4,3,2,1,0:T(8,128)(2,1)S(1)}, u32[]{:S(2)}, u32[]{:S(2)}) collective-permute-start(bf16[1,3,2,384,128]{4,3,2,1,0:T(8,128)(2,1)S(1)} %get-tuple-element.33), channel_id=1, source_target_pairs={{0,24},{8,0},{16,8},{24,16},{1,25},{9,1},{17,9},{25,17},{2,26},{10... | collective-permute-start | bytes 1769480 | tf_op jit(solution)/shard_map/ppermute | solution.py:227
  179.0 19.6 %collective-permute-start.9 = (bf16[1,2,384,128]{3,2,1,0:T(8,128)(2,1)}, bf16[1,2,384,128]{3,2,1,0:T(8,128)(2,1)}, u32[]{:S(2)}, u32[]{:S(2)}) collective-permute-start(bf16[1,2,384,128]{3,2,1,0:T(8,128)(2,1)} %get-tuple-element.55), channel_id=1, source_target_pairs={{0,24},{8,0},{16,8},{24,16},{1,25},{9,1},{17,9},{25,17},{2,26},{10... | collective-permute-start | bytes 589832 | tf_op jit(solution)/shard_map/ppermute | solution.py:246
  192.9 18.4 %collective-permute-start.10 = (bf16[1,2,384,128]{3,2,1,0:T(8,128)(2,1)}, bf16[1,2,384,128]{3,2,1,0:T(8,128)(2,1)}, u32[]{:S(2)}, u32[]{:S(2)}) collective-permute-start(bf16[1,2,384,128]{3,2,1,0:T(8,128)(2,1)} %get-tuple-element.54), channel_id=1, source_target_pairs={{0,16},{8,24},{16,0},{24,8},{1,17},{9,25},{17,1},{25,9},{2,18},{10... | collective-permute-start | bytes 589832 | tf_op jit(solution)/shard_map/ppermute | solution.py:246
  193.5 19.5 %collective-permute-start.11 = (bf16[1,2,384,128]{3,2,1,0:T(8,128)(2,1)}, bf16[1,2,384,128]{3,2,1,0:T(8,128)(2,1)S(1)}, u32[]{:S(2)}, u32[]{:S(2)}) collective-permute-start(bf16[1,2,384,128]{3,2,1,0:T(8,128)(2,1)} %get-tuple-element.52), channel_id=1, source_target_pairs={{0,8},{8,16},{16,24},{24,0},{1,9},{9,17},{17,25},{25,1},{2,10},{10... | collective-permute-start | bytes 589832 | tf_op jit(solution)/shard_map/ppermute | solution.py:246
  223.6 4.6 copy-start.17
  228.2 186.0 %reduce-scatter.7.cloned.1.call-start = ((), (), s32[]{:S(2)}) async-start(), calls=%async_computation.7 | async-start | bytes 7077888 | tf_op jit(solution)/shard_map/reduce_scatter | solution.py:219
  235.9 9.9 %copy-start.2 = (f32[8,4,16,768]{3,2,1,0:T(8,128)S(1)}, f32[8,4,16,768]{3,2,1,0:T(8,128)}, u32[]{:S(2)}) copy-start(f32[8,4,16,768]{3,2,1,0:T(8,128)} %fusion.41.refs_1_) | copy-start | bytes 4718596
  256.6 18.2 %collective-permute-start = (bf16[1,3,2,384,128]{4,3,2,1,0:T(8,128)(2,1)S(1)}, bf16[1,3,2,384,128]{4,3,2,1,0:T(8,128)(2,1)S(1)}, u32[]{:S(2)}, u32[]{:S(2)}) collective-permute-start(bf16[1,3,2,384,128]{4,3,2,1,0:T(8,128)(2,1)S(1)} %get-tuple-element.31), channel_id=1, source_target_pairs={{0,8},{8,16},{16,24},{24,0},{1,9},{9,17},{17,25},{25,1},{2,10},{10... | collective-permute-start | bytes 1769480 | tf_op jit(solution)/shard_map/ppermute | solution.py:227
  256.6 41.3 %collective-permute-start.1 = (bf16[1,3,2,384,128]{4,3,2,1,0:T(8,128)(2,1)S(1)}, bf16[1,3,2,384,128]{4,3,2,1,0:T(8,128)(2,1)S(1)}, u32[]{:S(2)}, u32[]{:S(2)}) collective-permute-start(bf16[1,3,2,384,128]{4,3,2,1,0:T(8,128)(2,1)S(1)} %get-tuple-element.30), channel_id=1, source_target_pairs={{0,16},{8,24},{16,0},{24,8},{1,17},{9,25},{17,1},{25,9},{2,18},{10... | collective-permute-start | bytes 1769480 | tf_op jit(solution)/shard_map/ppermute | solution.py:227
  256.7 41.3 %collective-permute-start.2 = (bf16[1,3,2,384,128]{4,3,2,1,0:T(8,128)(2,1)S(1)}, bf16[1,3,2,384,128]{4,3,2,1,0:T(8,128)(2,1)S(1)}, u32[]{:S(2)}, u32[]{:S(2)}) collective-permute-start(bf16[1,3,2,384,128]{4,3,2,1,0:T(8,128)(2,1)S(1)} %get-tuple-element.29), channel_id=1, source_target_pairs={{0,24},{8,0},{16,8},{24,16},{1,25},{9,1},{17,9},{25,17},{2,26},{10... | collective-permute-start | bytes 1769480 | tf_op jit(solution)/shard_map/ppermute | solution.py:227
  318.5 16.5 %collective-permute-start.3 = (bf16[1,2,384,128]{3,2,1,0:T(8,128)(2,1)S(1)}, bf16[1,2,384,128]{3,2,1,0:T(8,128)(2,1)S(1)}, u32[]{:S(2)}, u32[]{:S(2)}) collective-permute-start(bf16[1,2,384,128]{3,2,1,0:T(8,128)(2,1)S(1)} %get-tuple-element.49), channel_id=1, source_target_pairs={{0,24},{8,0},{16,8},{24,16},{1,25},{9,1},{17,9},{25,17},{2,26},{10... | collective-permute-start | bytes 589832 | tf_op jit(solution)/shard_map/ppermute | solution.py:246
  329.4 19.4 %collective-permute-start.4 = (bf16[1,2,384,128]{3,2,1,0:T(8,128)(2,1)S(1)}, bf16[1,2,384,128]{3,2,1,0:T(8,128)(2,1)S(1)}, u32[]{:S(2)}, u32[]{:S(2)}) collective-permute-start(bf16[1,2,384,128]{3,2,1,0:T(8,128)(2,1)S(1)} %get-tuple-element.48), channel_id=1, source_target_pairs={{0,16},{8,24},{16,0},{24,8},{1,17},{9,25},{17,1},{25,9},{2,18},{10... | collective-permute-start | bytes 589832 | tf_op jit(solution)/shard_map/ppermute | solution.py:246
  332.3 16.6 %collective-permute-start.5 = (bf16[1,2,384,128]{3,2,1,0:T(8,128)(2,1)S(1)}, bf16[1,2,384,128]{3,2,1,0:T(8,128)(2,1)S(1)}, u32[]{:S(2)}, u32[]{:S(2)}) collective-permute-start(bf16[1,2,384,128]{3,2,1,0:T(8,128)(2,1)S(1)} %get-tuple-element.46), channel_id=1, source_target_pairs={{0,8},{8,16},{16,24},{24,0},{1,9},{9,17},{17,25},{25,1},{2,10},{10... | collective-permute-start | bytes 589832 | tf_op jit(solution)/shard_map/ppermute | solution.py:246
  350.4 4.6 copy-start.18
  355.0 1.0 copy-start.23
  355.0 117.0 %all-gather.15.cloned.1.call-start = ((), (), s32[]{:S(2)}) async-start(), calls=%async_computation.12 | async-start | bytes 7077888 | tf_op jit(solution)/shard_map/all_gather | solution.py:216
  359.5 57.3 %copy-start.5 = (bf16[8,8,4,3072]{3,2,1,0:T(4,128)(2,1)S(1)}, bf16[8,8,4,3072]{3,2,1,0:T(4,128)(2,1)}, u32[]{:S(2)}) copy-start(bf16[8,8,4,3072]{3,2,1,0:T(4,128)(2,1)} %param.18) | copy-start | bytes 4718596
  426.4 2.7 copy-start.8
  426.4 2.7 copy-start.27
  426.4 93.1 %all-gather.11.cloned.1.call-start = ((), (), s32[]{:S(2)}) async-start(), calls=%async_computation.8 | async-start | bytes 7077888 | tf_op jit(solution)/shard_map/all_gather | solution.py:216
  429.2 2.7 slice-start.2
  431.8 137.5 %reduce-scatter.17.cloned.1.call-start = ((), (), s32[]{:S(2)}) async-start(), calls=%async_computation.15 | async-start | bytes 3538944 | tf_op jit(solution)/shard_map/reduce_scatter | solution.py:219
  436.0 1.4 copy-start.16
  436.0 1.4 slice-start.3
  436.1 183.0 %reduce-scatter.15.cloned.1.call-start = ((), (), s32[]{:S(2)}) async-start(), calls=%async_computation.14 | async-start | bytes 3538944 | tf_op jit(solution)/shard_map/reduce_scatter | solution.py:219
  440.2 244.1 %reduce-scatter.13.cloned.1.call-start = ((), (), s32[]{:S(2)}) async-start(), calls=%async_computation.13 | async-start | bytes 7077888 | tf_op jit(solution)/shard_map/reduce_scatter | solution.py:219
  491.6 258.0 %reduce-scatter.9.cloned.1.call-start = ((), (), s32[]{:S(2)}) async-start(), calls=%async_computation.9 | async-start | bytes 7077888 | tf_op jit(solution)/shard_map/reduce_scatter | solution.py:219
  539.0 2.9 copy-start.7
  541.9 1.7 copy-start.31
  541.9 1.8 copy-start.24
  541.9 77.2 %copy-start.25 = (f32[4,3072]{1,0:T(4,128)S(1)}, f32[4,3072]{1,0:T(4,128)}, u32[]{:S(2)}) copy-start(f32[4,3072]{1,0:T(4,128)} %get-tuple-element.56) | copy-start | bytes 147460
  541.9 77.2 %copy-start.26 = (f32[4,3072]{1,0:T(4,128)S(1)}, f32[4,3072]{1,0:T(4,128)}, u32[]{:S(2)}) copy-start(f32[4,3072]{1,0:T(4,128)} %get-tuple-element.61) | copy-start | bytes 147460
  621.7 65.2 %copy-start.11 = (bf16[4,8,4,3072]{3,2,1,0:T(4,128)(2,1)S(1)}, bf16[4,8,4,3072]{3,2,1,0:T(4,128)(2,1)}, u32[]{:S(2)}) copy-start(bf16[4,8,4,3072]{3,2,1,0:T(4,128)(2,1)} %get-tuple-element.39) | copy-start | bytes 2359300
  621.7 65.2 %copy-start.22 = (f32[4,3072]{1,0:T(4,128)S(1)}, f32[4,3072]{1,0:T(4,128)}, u32[]{:S(2)}) copy-start(f32[4,3072]{1,0:T(4,128)} %get-tuple-element.67) | copy-start | bytes 147460
  686.8 5.2 copy-start.12
  692.0 2.8 copy-start.19
  694.9 57.5 %copy-start.10 = (bf16[4,8,4,3072]{3,2,1,0:T(4,128)(2,1)S(1)}, bf16[4,8,4,3072]{3,2,1,0:T(4,128)(2,1)}, u32[]{:S(2)}) copy-start(bf16[4,8,4,3072]{3,2,1,0:T(4,128)(2,1)} %get-tuple-element.25) | copy-start | bytes 2359300
  752.4 5.2 copy-start.13
  759.8 7.5 copy-start.14
  759.8 7.5 copy-start.15
  762.7 6.9 collective-permute-start.12
  766.1 5.5 collective-permute-start.13
Sparse Core Ops, SparseCore 0:
  12.6 35.0 all-gather.18
  49.5 45.5 all-gather.12
  96.9 32.3 all-gather.16
  131.6 45.5 all-gather.8
  228.3 58.9 reduce-scatter.10
  355.2 58.9 reduce-scatter.6
  426.5 45.4 all-gather.14
  474.0 45.5 all-gather.10
  522.9 46.2 reduce-scatter.16
  572.8 46.2 reduce-scatter.14
  622.5 61.7 reduce-scatter.12
  687.8 61.7 reduce-scatter.8
